TPU v7x, 32 devices: a whole 2x2x4 slice. The times are simulated.
32 devices in a mesh: grp: 2 (over y), row: 16 (over z, x, core), kc: 1.
Axes of the slice: x: 2, y: 2, z: 4, core: 2. Of those that a mesh axis runs over, the one named last changes fastest.
Arguments:
- pair: bfloat16 [256, 128, 128], P(('grp', 'row'), 'kc'), parts along dimension 0, may hold values from -6 to 6
- w_in: bfloat16 [2, 128, 512], replicated, may hold values from -0.5 to 0.5
- w_gate: bfloat16 [2, 128, 128], replicated, may hold values from -0.5 to 0.5
- w_out: bfloat16 [2, 128, 128], replicated, may hold values from -0.5 to 0.5
- gain_in: float32 [2, 128], replicated, may hold values from 0.25 to 1.75
- bias_in: float32 [2, 128], replicated, may hold values from -0.6 to 0.6
- gain_mid: float32 [2, 128], replicated, may hold values from 0.25 to 1.75
- bias_mid: float32 [2, 128], replicated, may hold values from -0.6 to 0.6
Outputs:
- updated: bfloat16 [256, 128, 128], P(('grp', 'row'), 'kc'), parts along dimension 0
- incoming_mid: bfloat16 [256, 128, 128], P(('grp', 'row'), 'kc'), parts along dimension 0
There are 2 independent parts, one for each index of `grp`. A program takes and returns all parts, laid end to end along the dimension named above; an argument that names none is the same for every part. Nothing has to cross between parts.
All inputs are finite; a program needn't handle non-finite values.
Results may differ from a plain program's by a relative error of at most 0.025.
Values may be sent and summed in bfloat16 or wider, within the bound.
A program may use at most 64 MiB of HBM per device.

v0:
```python
import jax
import jax.numpy as jnp
from jax import lax
from jax.sharding import PartitionSpec as P


def layer_norm(values, gain, bias, axis_pos):
    center = jnp.mean(values, axis=axis_pos, keepdims=True)
    spread = jnp.mean((values - center) ** 2, axis=axis_pos, keepdims=True)
    return (values - center) * lax.rsqrt(spread + 1e-05) * gain + bias


def prepare(state, layer_index, w_in, w_gate, gain_in, bias_in):
    hidden = w_in.shape[2] // 4
    pair_float = state.astype(jnp.float32)
    normed = layer_norm(pair_float, gain_in[layer_index], bias_in[layer_index], 2).astype(
        jnp.bfloat16
    )
    projected = jnp.einsum(
        "ijc,ch->hij", normed, w_in[layer_index], preferred_element_type=jnp.float32
    )
    left = (jax.nn.sigmoid(projected[:hidden]) * projected[hidden : 2 * hidden]).astype(
        jnp.bfloat16
    )
    right = (jax.nn.sigmoid(projected[2 * hidden : 3 * hidden]) * projected[3 * hidden :]).astype(
        jnp.bfloat16
    )
    gate_values = jax.nn.sigmoid(
        jnp.einsum("ijc,cd->ijd", normed, w_gate[layer_index], preferred_element_type=jnp.float32)
    )
    return (pair_float, left, right, gate_values)


def finish(pair_float, gate_values, returned, layer_index, w_out, gain_mid, bias_mid):
    middle = layer_norm(
        returned.astype(jnp.float32),
        gain_mid[layer_index][:, None],
        bias_mid[layer_index][:, None],
        1,
    ).astype(jnp.bfloat16)
    branch = jnp.einsum(
        "jhi,hc->ijc", middle, w_out[layer_index], preferred_element_type=jnp.float32
    )
    return ((pair_float + gate_values * branch).astype(jnp.bfloat16), middle)


def shards(pair, w_in, w_gate, w_out, gain_in, bias_in, gain_mid, bias_mid):
    pair_float, left, right, gate_values = prepare(pair, 0, w_in, w_gate, gain_in, bias_in)
    left_c, right_c = (
        lax.all_to_all(left, "row", split_axis=0, concat_axis=1, tiled=True),
        lax.all_to_all(right, "row", split_axis=0, concat_axis=1, tiled=True),
    )
    right_rows = right_c
    summed = lax.psum_scatter(
        jnp.einsum("hjs,his->jhi", right_rows, left_c, preferred_element_type=jnp.float32).astype(
            jnp.bfloat16
        ),
        "kc",
        scatter_dimension=0,
        tiled=True,
    ).astype(jnp.float32)
    returned = lax.all_to_all(
        summed.astype(jnp.bfloat16), "row", split_axis=2, concat_axis=1, tiled=True
    )
    state, unused = finish(pair_float, gate_values, returned, 0, w_out, gain_mid, bias_mid)
    pair_float, left, right, gate_values = prepare(state, 1, w_in, w_gate, gain_in, bias_in)
    left_c, right_c = (
        lax.all_to_all(left, "row", split_axis=0, concat_axis=1, tiled=True),
        lax.all_to_all(right, "row", split_axis=0, concat_axis=1, tiled=True),
    )
    summed = jnp.einsum(
        "hpj,hpi->jhi",
        right_c,
        lax.all_gather(left_c, "kc", axis=2, tiled=True),
        preferred_element_type=jnp.float32,
    )
    returned = lax.all_to_all(
        summed.astype(jnp.bfloat16), "row", split_axis=2, concat_axis=1, tiled=True
    )
    final_state, middle = finish(pair_float, gate_values, returned, 1, w_out, gain_mid, bias_mid)
    return (final_state, middle.transpose(2, 0, 1))


def solution(mesh):
    in_specs = (P(("grp", "row"), "kc", None), P(), P(), P(), P(), P(), P(), P())
    out_specs = (P(("grp", "row"), "kc", None), P(("grp", "row"), "kc", None))
    return jax.shard_map(shards, mesh=mesh, in_specs=in_specs, out_specs=out_specs, check_vma=False)
```

profile of v0, /device:TPU:0, one launch (start us, length us, event | category | flops | bytes accessed | tf_op | source)
XLA Modules:
  0.0 97.4 jit_solution(11547588254969075623)
XLA Ops:
  0.6 1.1 %copy.79 = bf16[8,128,128]{1,2,0:T(8,128)(2,1)S(1)} copy(bf16[8,128,128]{2,1,0:T(8,128)(2,1)} %param.8) | data formatting | bytes 524288 | tf_op args[0]
  1.8 0.1 fusion.17
  1.9 0.8 slice_bitcast_fusion
  2.7 1.4 %convolution_bitcast_fusion.1 = f32[512,8,128]{0,2,1:T(8,128)S(1)} fusion(bf16[2,128,512]{2,1,0:T(8,128)(2,1)} %param.9, bf16[8,128,128]{1,2,0:T(8,128)(2,1)S(1)} %copy.79, f32[128]{0:T(128)S(1)} %get-tuple-element.23, f32[128]{0:T(128)S(1)} %get-tuple-element.26, f32[8,128]{1,0:T(8,128)S(1)} %add_rsqrt_fusion.3, f32[8,128]{1,0:T(8,128)S(1)} %broadcast_multiply_fusion.3), kind=kOutput, calls=%fused_computation.1 | convolution fusion | flops 135004160 | bytes 2499584 | tf_op jit(solution)/shard_map/ijc,ch->hij/dot_general | solution.py:19
  4.1 0.3 fusion.33
  4.5 0.9 copy.85
  5.3 7.4 %all-to-all-start.1 = ((bf16[128,8,128]{2,1,0:T(8,128)(2,1)}), bf16[128,8,128]{2,1,0:T(8,128)(2,1)S(1)}, u32[]{:S(2)}, u32[]{:S(2)}) async-start(bf16[128,8,128]{2,1,0:T(8,128)(2,1)} %copy.85), calls=%async_computation.1 | async-start | bytes 524288 | tf_op jit(solution)/shard_map/all_to_all | solution.py:51
  12.7 0.2 copy.83
  12.9 9.9 %all-to-all-done.1 = bf16[128,8,128]{2,1,0:T(8,128)(2,1)S(1)} async-done(((bf16[128,8,128]{2,1,0:T(8,128)(2,1)}), bf16[128,8,128]{2,1,0:T(8,128)(2,1)S(1)}, u32[]{:S(2)}, u32[]{:S(2)}) %all-to-all-start.1) | async-done | bytes 262176 | tf_op jit(solution)/shard_map/all_to_all | solution.py:51
  22.7 12.8 %all_to_all.90 = bf16[128,8,128]{2,1,0:T(8,128)(2,1)S(1)} all-to-all(bf16[128,8,128]{2,1,0:T(8,128)(2,1)S(1)} %copy.83), channel_id=1, replica_groups=mesh['grp'=2,'row'=16,'kc'=1] {'row'}, dimensions={0} | all-to-all | bytes 524288 | tf_op jit(solution)/shard_map/all_to_all | solution.py:50
  35.6 0.3 fusion.13
  35.9 0.9 copy.87
  36.7 3.5 %all-to-all-start.2 = ((bf16[128,8,128]{0,1,2:T(8,128)(2,1)}), bf16[128,8,128]{0,1,2:T(8,128)(2,1)S(1)}, u32[]{:S(2)}, u32[]{:S(2)}) async-start(bf16[128,8,128]{0,1,2:T(8,128)(2,1)} %copy.87), calls=%async_computation.2 | async-start | bytes 524288 | tf_op jit(solution)/shard_map/all_to_all | solution.py:62
  40.3 0.1 mul.113
  40.4 0.1 copy.89
  40.5 0.1 add.113
  40.6 0.1 copy.90
  40.6 0.4 fusion.2
  41.1 9.2 %all-to-all-done.2 = bf16[128,8,128]{0,1,2:T(8,128)(2,1)S(1)} async-done(((bf16[128,8,128]{0,1,2:T(8,128)(2,1)}), bf16[128,8,128]{0,1,2:T(8,128)(2,1)S(1)}, u32[]{:S(2)}, u32[]{:S(2)}) %all-to-all-start.2) | async-done | bytes 262176 | tf_op jit(solution)/shard_map/all_to_all | solution.py:62
  50.3 0.1 fusion.42
  50.4 0.1 fusion.45
  50.6 0.3 fusion.48
  50.9 0.1 copy.91
  51.0 0.3 fusion.74
  51.3 0.1 multiply_reduce_fusion.1
  51.4 0.5 convolution_bitcast_fusion
  51.9 0.3 fusion.25
  52.2 0.9 copy.97
  53.1 3.5 %all-to-all-start.3 = ((bf16[128,8,128]{2,1,0:T(8,128)(2,1)}), bf16[128,8,128]{2,1,0:T(8,128)(2,1)S(1)}, u32[]{:S(2)}, u32[]{:S(2)}) async-start(bf16[128,8,128]{2,1,0:T(8,128)(2,1)} %copy.97), calls=%async_computation.3 | async-start | bytes 524288 | tf_op jit(solution)/shard_map/all_to_all | solution.py:68
  56.7 0.2 copy.99
  56.8 9.8 %all-to-all-done.3 = bf16[128,8,128]{2,1,0:T(8,128)(2,1)S(1)} async-done(((bf16[128,8,128]{2,1,0:T(8,128)(2,1)}), bf16[128,8,128]{2,1,0:T(8,128)(2,1)S(1)}, u32[]{:S(2)}, u32[]{:S(2)}) %all-to-all-start.3) | async-done | bytes 262176 | tf_op jit(solution)/shard_map/all_to_all | solution.py:68
  66.7 12.8 %all_to_all.91 = bf16[128,8,128]{2,1,0:T(8,128)(2,1)S(1)} all-to-all(bf16[128,8,128]{2,1,0:T(8,128)(2,1)S(1)} %copy.99), channel_id=1, replica_groups=mesh['grp'=2,'row'=16,'kc'=1] {'row'}, dimensions={0} | all-to-all | bytes 524288 | tf_op jit(solution)/shard_map/all_to_all | solution.py:69
  79.5 0.3 fusion.14
  79.8 0.9 copy.102
  80.6 3.5 %all-to-all-start.5 = ((bf16[128,8,128]{0,1,2:T(8,128)(2,1)}), bf16[128,8,128]{0,1,2:T(8,128)(2,1)S(1)}, u32[]{:S(2)}, u32[]{:S(2)}) async-start(bf16[128,8,128]{0,1,2:T(8,128)(2,1)} %copy.102), calls=%async_computation.5 | async-start | bytes 524288 | tf_op jit(solution)/shard_map/all_to_all | solution.py:77
  84.2 0.1 mul.126
  84.3 0.1 copy.104
  84.3 0.1 add.125
  84.4 0.1 copy.105
  84.5 0.4 fusion.6
  84.9 9.3 %all-to-all-done.5 = bf16[128,8,128]{0,1,2:T(8,128)(2,1)S(1)} async-done(((bf16[128,8,128]{0,1,2:T(8,128)(2,1)}), bf16[128,8,128]{0,1,2:T(8,128)(2,1)S(1)}, u32[]{:S(2)}, u32[]{:S(2)}) %all-to-all-start.5) | async-done | bytes 262176 | tf_op jit(solution)/shard_map/all_to_all | solution.py:77
  94.3 0.1 fusion.49
  94.4 0.1 multiply_reduce_fusion
  94.6 0.3 fusion.40
  94.9 0.9 copy.111
  95.8 0.3 add_convert_fusion
  96.2 0.3 fusion.10
  96.5 0.9 copy.110
  (23 shorter events, 0.3 us)
Async XLA Ops:
  4.4 35.9 %copy-start.2 = (f32[2,128]{1,0:T(2,128)S(1)}, f32[2,128]{1,0:T(2,128)}, u32[]{:S(2)}) copy-start(f32[2,128]{1,0:T(2,128)} %param.15) | copy-start | bytes 3076
  4.4 35.9 %copy-start.3 = (f32[2,128]{1,0:T(2,128)S(1)}, f32[2,128]{1,0:T(2,128)}, u32[]{:S(2)}) copy-start(f32[2,128]{1,0:T(2,128)} %param.14) | copy-start | bytes 3076
  4.4 36.2 %copy-start.4 = (bf16[2,128,128]{2,1,0:T(8,128)(2,1)S(1)}, bf16[2,128,128]{2,1,0:T(8,128)(2,1)}, u32[]{:S(2)}) copy-start(bf16[2,128,128]{2,1,0:T(8,128)(2,1)} %param.10) | copy-start | bytes 196612
  5.3 17.4 %all-to-all-start.1 = ((bf16[128,8,128]{2,1,0:T(8,128)(2,1)}), bf16[128,8,128]{2,1,0:T(8,128)(2,1)S(1)}, u32[]{:S(2)}, u32[]{:S(2)}) async-start(bf16[128,8,128]{2,1,0:T(8,128)(2,1)} %copy.85), calls=%async_computation.1 | async-start | bytes 524288 | tf_op jit(solution)/shard_map/all_to_all | solution.py:51
  36.7 13.5 %all-to-all-start.2 = ((bf16[128,8,128]{0,1,2:T(8,128)(2,1)}), bf16[128,8,128]{0,1,2:T(8,128)(2,1)S(1)}, u32[]{:S(2)}, u32[]{:S(2)}) async-start(bf16[128,8,128]{0,1,2:T(8,128)(2,1)} %copy.87), calls=%async_computation.2 | async-start | bytes 524288 | tf_op jit(solution)/shard_map/all_to_all | solution.py:62
  40.6 10.4 %copy-start.1 = (bf16[2,128,128]{2,1,0:T(8,128)(2,1)S(1)}, bf16[2,128,128]{2,1,0:T(8,128)(2,1)}, u32[]{:S(2)}) copy-start(bf16[2,128,128]{2,1,0:T(8,128)(2,1)} %param.11) | copy-start | bytes 196612
  41.0 10.3 %copy-start = (bf16[2,128,512]{2,1,0:T(8,128)(2,1)S(1)}, bf16[2,128,512]{2,1,0:T(8,128)(2,1)}, u32[]{:S(2)}) copy-start(bf16[2,128,512]{2,1,0:T(8,128)(2,1)} %param.9) | copy-start | bytes 786436
  53.1 13.5 %all-to-all-start.3 = ((bf16[128,8,128]{2,1,0:T(8,128)(2,1)}), bf16[128,8,128]{2,1,0:T(8,128)(2,1)S(1)}, u32[]{:S(2)}, u32[]{:S(2)}) async-start(bf16[128,8,128]{2,1,0:T(8,128)(2,1)} %copy.97), calls=%async_computation.3 | async-start | bytes 524288 | tf_op jit(solution)/shard_map/all_to_all | solution.py:68
  80.6 13.5 %all-to-all-start.5 = ((bf16[128,8,128]{0,1,2:T(8,128)(2,1)}), bf16[128,8,128]{0,1,2:T(8,128)(2,1)S(1)}, u32[]{:S(2)}, u32[]{:S(2)}) async-start(bf16[128,8,128]{0,1,2:T(8,128)(2,1)} %copy.102), calls=%async_computation.5 | async-start | bytes 524288 | tf_op jit(solution)/shard_map/all_to_all | solution.py:77
where the time goes:
time: 98.1 us; the launch traced here: 97.4 us
  waiting for transfers between devices  38.2 us (39%)
  blocking collectives  25.6 us (26%)
  starting transfers between devices  18 us (18%)
  local copies, waits for them, and re-layouts  8.37 us (9%)
  matrix products  3.9 us (4%)
  other arithmetic  2.41 us (2%)
    all_to_all x2, waiting for transfers between devices, shards(): lax.all_to_all(summed.astype(jnp.bfloat16), 'row', split_axis=2, concat_a...  18.5 us
    all_to_all x1, blocking collectives, shards(): lax.all_to_all(right, 'row', split_axis=0, concat_axis=1, tiled=True)  12.8 us
    all_to_all x1, blocking collectives, shards(): lax.all_to_all(left, 'row', split_axis=0, concat_axis=1, tiled=True)  12.8 us
    all_to_all x1, waiting for transfers between devices, shards(): lax.all_to_all(right, 'row', split_axis=0, concat_axis=1, tiled=True)  9.85 us
    all_to_all x1, waiting for transfers between devices, shards(): lax.all_to_all(left, 'row', split_axis=0, concat_axis=1, tiled=True)  9.81 us
    all_to_all x1, starting transfers between devices, shards(): lax.all_to_all(right, 'row', split_axis=0, concat_axis=1, tiled=True)  7.36 us
    all_to_all x2, starting transfers between devices, shards(): lax.all_to_all(summed.astype(jnp.bfloat16), 'row', split_axis=2, concat_a...  7.07 us
    all_to_all x1, starting transfers between devices, shards(): lax.all_to_all(left, 'row', split_axis=0, concat_axis=1, tiled=True)  3.53 us
  transfers between devices with their start and end apart: 4, of which 4 were waited for; matrix products, arithmetic and copies ran while one was open for 2% of the time, Pallas kernels for 0%

commit v1 on v0

--- a/solution.py
+++ b/solution.py
@@ -1,6 +1,10 @@
+import functools
+
 import jax
 import jax.numpy as jnp
 from jax import lax
+from jax.experimental import pallas as pl
+from jax.experimental.pallas import tpu as pltpu
 from jax.sharding import PartitionSpec as P
 
 
@@ -80,8 +84,224 @@
     final_state, middle = finish(pair_float, gate_values, returned, 1, w_out, gain_mid, bias_mid)
     return (final_state, middle.transpose(2, 0, 1))
 
+MESH = pl.DeviceIdType.MESH
+F32 = jnp.float32
+BF16 = jnp.bfloat16
+
+
+def sigmoid(x):
+    return 0.5 * jnp.tanh(0.5 * x) + 0.5
+
+
+def norm_lanes(x, gain, bias):
+    center = jnp.mean(x, axis=-1, keepdims=True)
+    moved = x - center
+    spread = jnp.mean(moved * moved, axis=-1, keepdims=True)
+    return moved * lax.rsqrt(spread + 1e-05) * gain + bias
+
+
+def fused_kernel(
+    n,
+    pair_ref,
+    w_in_ref,
+    w_gate_ref,
+    w_out_ref,
+    gain_in_ref,
+    bias_in_ref,
+    gain_mid_ref,
+    bias_mid_ref,
+    out_ref,
+    mid_ref,
+    w_t,
+    state,
+    normed,
+    gate,
+    lanes_l,
+    lanes_r,
+    send_a,
+    recv_a,
+    send_b,
+    recv_b,
+    sa_sem,
+    ra_sem,
+    sb_sem,
+    rb_sem,
+):
+    rows, tokens, channels = pair_ref.shape
+    hidden = w_out_ref.shape[1]
+    hb = hidden // n
+    part = hb * rows
+    me = lax.axis_index("row")
+
+    barrier = pltpu.get_barrier_semaphore()
+
+    def greet(o, c):
+        pl.semaphore_signal(
+            barrier, inc=1, device_id={"row": lax.rem(me + o, n)}, device_id_type=MESH
+        )
+        return c
+
+    lax.fori_loop(1, n, greet, 0)
+
+    def copy_to(send, recv, ssem, rsem, u, other):
+        return pltpu.make_async_remote_copy(
+            src_ref=send.at[u, other],
+            dst_ref=recv.at[u, me],
+            send_sem=ssem.at[u, other],
+            recv_sem=rsem.at[u, me],
+            device_id={"row": other},
+            device_id_type=MESH,
+        )
+
+    def copy_from(send, recv, ssem, rsem, u, other):
+        return pltpu.make_async_remote_copy(
+            src_ref=send.at[u, other],
+            dst_ref=recv.at[u, other],
+            send_sem=ssem.at[u, other],
+            recv_sem=rsem.at[u, other],
+            device_id={"row": other},
+            device_id_type=MESH,
+        )
+
+    def start_all(bufs, u):
+        def body(o, c):
+            copy_to(*bufs, u, lax.rem(me + o, n)).start()
+            return c
+
+        lax.fori_loop(1, n, body, 0)
+
+    def wait_all(bufs, u):
+        def body(o, c):
+            copy_from(*bufs, u, lax.rem(me + n - o, n)).wait_recv()
+            return c
+
+        lax.fori_loop(1, n, body, 0)
+
+    def drain(bufs, u):
+        def body(o, c):
+            copy_to(*bufs, u, lax.rem(me + o, n)).wait_send()
+            return c
+
+        lax.fori_loop(1, n, body, 0)
+
+    bufs_a = (send_a, recv_a, sa_sem, ra_sem)
+    bufs_b = (send_b, recv_b, sb_sem, rb_sem)
+
+    for u in range(2):
+        w_t[u] = w_in_ref[u].T
+
+    for u in range(2):
+        source = pair_ref if u == 0 else state
+        for i in range(rows):
+            x = source[i].astype(F32)
+            nrm = norm_lanes(x, gain_in_ref[u : u + 1, :], bias_in_ref[u : u + 1, :]).astype(BF16)
+            normed[i] = nrm
+            proj = lax.dot_general(
+                w_t[u], nrm, (((1,), (1,)), ((), ())), preferred_element_type=F32
+            )
+            lanes_l[pl.ds(i, hidden, stride=rows), :] = (
+                sigmoid(proj[:hidden]) * proj[hidden : 2 * hidden]
+            )
+            lanes_r[pl.ds(i, hidden, stride=rows), :] = (
+                sigmoid(proj[2 * hidden : 3 * hidden]) * proj[3 * hidden :]
+            )
+        send_a[u, :, :part, :] = lanes_l[...].reshape(n, part, tokens).astype(BF16)
+        send_a[u, :, part:, :] = lanes_r[...].reshape(n, part, tokens).astype(BF16)
+        if u == 0:
+            pl.semaphore_wait(barrier, n - 1)
+        start_all(bufs_a, u)
+        recv_a[u, pl.ds(me, 1)] = send_a[u, pl.ds(me, 1)]
+        for i in range(rows):
+            gate[i] = sigmoid(jnp.dot(normed[i], w_gate_ref[u], preferred_element_type=F32))
+        wait_all(bufs_a, u)
+        dims = (((1,), (1,)), ((), ())) if u == 0 else (((0,), (0,)), ((), ()))
+        for p in range(hb // 2):
+            lo = 2 * p * rows
+            lblk = recv_a[u, :, lo : lo + 2 * rows, :].astype(F32)
+            rblk = recv_a[u, :, part + lo : part + lo + 2 * rows, :].astype(F32)
+            for q in range(2):
+                cut = slice(q * rows, (q + 1) * rows)
+                lh = lblk[:, cut, :].reshape(n * rows, tokens).astype(BF16)
+                rh = rblk[:, cut, :].reshape(n * rows, tokens).astype(BF16)
+                tri = lax.dot_general(lh, rh, dims, preferred_element_type=F32)
+                lanes_l[pl.ds(2 * p + q, n * rows, stride=hb), :] = tri
+        send_b[u] = lanes_l[...].reshape(n, part, tokens).astype(BF16)
+        start_all(bufs_b, u)
+        recv_b[u, pl.ds(me, 1)] = send_b[u, pl.ds(me, 1)]
+        wait_all(bufs_b, u)
+        for p in range(rows // 2):
+            lo = 2 * p * hb
+            blk = recv_b[u, :, lo : lo + 2 * hb, :].astype(F32)
+            for q in range(2):
+                i = 2 * p + q
+                tri = blk[:, q * hb : (q + 1) * hb, :].reshape(hidden, tokens).T
+                mid = norm_lanes(
+                    tri, gain_mid_ref[u : u + 1, :], bias_mid_ref[u : u + 1, :]
+                ).astype(BF16)
+                branch = jnp.dot(mid, w_out_ref[u], preferred_element_type=F32)
+                new = (source[i].astype(F32) + gate[i] * branch).astype(BF16)
+                if u == 0:
+                    state[i] = new
+                else:
+                    out_ref[i] = new
+                    mid_ref[i] = mid
+    for u in range(2):
+        drain(bufs_a, u)
+        drain(bufs_b, u)
+
+
+def fused(n, *operands):
+    pair, hidden = operands[0], operands[3].shape[1]
+    rows, tokens, channels = pair.shape
+    part = hidden // n * rows
+    vmem = pl.BlockSpec(memory_space=pltpu.VMEM)
+    return pl.pallas_call(
+        functools.partial(fused_kernel, n),
+        out_shape=(
+            jax.ShapeDtypeStruct(pair.shape, BF16),
+            jax.ShapeDtypeStruct((rows, tokens, hidden), BF16),
+        ),
+        in_specs=[vmem] * len(operands),
+        out_specs=(vmem, vmem),
+        scratch_shapes=[
+            pltpu.VMEM((2, 4 * hidden, channels), BF16),
+            pltpu.VMEM(pair.shape, BF16),
+            pltpu.VMEM(pair.shape, BF16),
+            pltpu.VMEM(pair.shape, F32),
+            pltpu.VMEM((hidden * rows, tokens), F32),
+            pltpu.VMEM((hidden * rows, tokens), F32),
+            pltpu.VMEM((2, n, 2 * part, tokens), BF16),
+            pltpu.VMEM((2, n, 2 * part, tokens), BF16),
+            pltpu.VMEM((2, n, part, tokens), BF16),
+            pltpu.VMEM((2, n, part, tokens), BF16),
+        ]
+        + [pltpu.SemaphoreType.DMA((2, n))] * 4,
+        compiler_params=pltpu.CompilerParams(
+            collective_id=0, has_side_effects=True, vmem_limit_bytes=48 * 2**20
+        ),
+    )(*operands)
+
+
+def fits(mesh, pair_shape, hidden):
+    n = mesh.shape["row"]
+    rows = pair_shape[0] // (n * mesh.shape["grp"])
+    tokens = pair_shape[1]
+    aligned = rows % 8 == 0 and hidden % (8 * n) == 0 and tokens % 128 == 0
+    small = hidden * rows * tokens * 40 <= 40 * 2**20
+    return mesh.shape["kc"] == 1 and n > 1 and n * rows == tokens and aligned and small
+
 
 def solution(mesh):
     in_specs = (P(("grp", "row"), "kc", None), P(), P(), P(), P(), P(), P(), P())
     out_specs = (P(("grp", "row"), "kc", None), P(("grp", "row"), "kc", None))
-    return jax.shard_map(shards, mesh=mesh, in_specs=in_specs, out_specs=out_specs, check_vma=False)
+
+    def run(*operands):
+        if fits(mesh, operands[0].shape, operands[3].shape[1]):
+            body = functools.partial(fused, mesh.shape["row"])
+        else:
+            body = shards
+        return jax.shard_map(
+            body, mesh=mesh, in_specs=in_specs, out_specs=out_specs, check_vma=False
+        )(*operands)
+
+    return run

time: 98.1 us -> 57 us (0.58)
  Pallas kernels: 0 us -> 48.2 us
  waiting for transfers between devices: 38.2 us -> 0 us
  blocking collectives: 25.6 us -> 0 us
  starting transfers between devices: 18 us -> 0 us
  matrix products: 3.9 us -> 0 us
  other arithmetic: 2.41 us -> 0 us
    pallas_call x0 -> x1, Pallas kernels: none -> 48.2 us  [fused(): pl.pallas_call(functools.partial(fused_kernel, n), out_shape=(jax.ShapeDt...]
    all_to_all x4 -> x0, waiting for transfers between devices: 38.2 us -> none  [the longest x2 18.5 us: shards(): lax.all_to_all(summed.astype(jnp.bfloat16), 'row', split_axis=2, concat_a...]
    all_to_all x2 -> x0, blocking collectives: 25.6 us -> none  [the longest x1 12.8 us: shards(): lax.all_to_all(right, 'row', split_axis=0, concat_axis=1, tiled=True)]
    all_to_all x4 -> x0, starting transfers between devices: 18 us -> none  [the longest x1 7.36 us: shards(): lax.all_to_all(right, 'row', split_axis=0, concat_axis=1, tiled=True)]
    unnamed x13 -> x18, local copies, waits for them, and re-layouts: 2.9 us -> 7.69 us
    convert_element_type x9 -> x0, local copies, waits for them, and re-layouts: 4.06 us -> none  [the longest x2 1.07 us: prepare(): (jax.nn.sigmoid(projected[:hidden]) * projected[hidden:2 * hidden]).astyp...]
    dot_general x8 -> x0, matrix products: 3.9 us -> none  [the longest x2 1.98 us: prepare(): jnp.einsum('ijc,ch->hij', normed, w_in[layer_index], preferred_element_ty...]
    convert_element_type x6 -> x0, other arithmetic: 1.62 us -> none  [the longest x3 1.01 us: finish(): middle = layer_norm(returned.astype(jnp.float32), gain_mid[layer_index][:...]
  transfers between devices with their start and end apart: 4 -> 0, of which waited for: 4 -> 0; matrix products, arithmetic and copies ran while one was open for 2% -> 0% of each run, Pallas kernels for 0% -> 0%
where the time goes in v1:
time: 57 us; the launch traced here: 56.6 us
  Pallas kernels  48.2 us (85%)
  local copies, waits for them, and re-layouts  7.69 us (13%)
  between operations  0.66 us (1%)
    pallas_call x1, Pallas kernels, fused(): pl.pallas_call(functools.partial(fused_kernel, n), out_shape=(jax.ShapeDt...  48.2 us
    unnamed x18, local copies, waits for them, and re-layouts  7.69 us

profile of v1, /device:TPU:0, one launch (start us, length us, event | category | flops | bytes accessed | tf_op | source)
XLA Modules:
  0.0 56.6 jit_solution(2297413741169301411)
XLA Ops:
  0.6 0.0 copy-start
  0.6 0.9 %copy-done = bf16[8,128,128]{2,1,0:T(8,128)(2,1)S(1)} copy-done((bf16[8,128,128]{2,1,0:T(8,128)(2,1)S(1)}, bf16[8,128,128]{2,1,0:T(8,128)(2,1)}, u32[]{:S(2)}) %copy-start) | copy-done | bytes 262168
  1.6 0.0 copy-start.1
  1.6 0.9 %copy-done.1 = bf16[2,128,512]{2,1,0:T(8,128)(2,1)S(1)} copy-done((bf16[2,128,512]{2,1,0:T(8,128)(2,1)S(1)}, bf16[2,128,512]{2,1,0:T(8,128)(2,1)}, u32[]{:S(2)}) %copy-start.1) | copy-done | bytes 262168
  2.5 0.0 copy-start.2
  2.5 0.8 %copy-done.2 = bf16[2,128,128]{2,1,0:T(8,128)(2,1)S(1)} copy-done((bf16[2,128,128]{2,1,0:T(8,128)(2,1)S(1)}, bf16[2,128,128]{2,1,0:T(8,128)(2,1)}, u32[]{:S(2)}) %copy-start.2) | copy-done | bytes 65560
  3.4 0.0 copy-start.3
  3.4 0.8 %copy-done.3 = bf16[2,128,128]{2,1,0:T(8,128)(2,1)S(1)} copy-done((bf16[2,128,128]{2,1,0:T(8,128)(2,1)S(1)}, bf16[2,128,128]{2,1,0:T(8,128)(2,1)}, u32[]{:S(2)}) %copy-start.3) | copy-done | bytes 65560
  4.2 0.0 copy-start.4
  4.2 0.7 %copy-done.4 = f32[2,128]{1,0:T(2,128)S(1)} copy-done((f32[2,128]{1,0:T(2,128)S(1)}, f32[2,128]{1,0:T(2,128)}, u32[]{:S(2)}) %copy-start.4) | copy-done | bytes 1048
  4.9 0.0 copy-start.5
  4.9 0.7 %copy-done.5 = f32[2,128]{1,0:T(2,128)S(1)} copy-done((f32[2,128]{1,0:T(2,128)S(1)}, f32[2,128]{1,0:T(2,128)}, u32[]{:S(2)}) %copy-start.5) | copy-done | bytes 1048
  5.6 0.0 copy-start.6
  5.6 0.7 %copy-done.6 = f32[2,128]{1,0:T(2,128)S(1)} copy-done((f32[2,128]{1,0:T(2,128)S(1)}, f32[2,128]{1,0:T(2,128)}, u32[]{:S(2)}) %copy-start.6) | copy-done | bytes 1048
  6.3 0.0 copy-start.7
  6.3 0.7 %copy-done.7 = f32[2,128]{1,0:T(2,128)S(1)} copy-done((f32[2,128]{1,0:T(2,128)S(1)}, f32[2,128]{1,0:T(2,128)}, u32[]{:S(2)}) %copy-start.7) | copy-done | bytes 1048
  6.9 48.2 %shard_map.95 = (bf16[8,128,128]{2,1,0:T(8,128)(2,1)S(1)}, bf16[8,128,128]{2,1,0:T(8,128)(2,1)S(1)}) custom-call(bf16[8,128,128]{2,1,0:T(8,128)(2,1)S(1)} %copy-done, bf16[2,128,512]{2,1,0:T(8,128)(2,1)S(1)} %copy-done.1, bf16[2,128,128]{2,1,0:T(8,128)(2,1)S(1)} %copy-done.2, bf16[2,128,128]{2,1,0:T(8,128)(2,1)S(1)} %copy-done.3, f32[2,128]{1,0:T(2,128)S(1)} %copy-done.4, ...), custom_call_target="tpu_custom_call" | custom-call | tf_op jit(solution)/shard_map/pallas_call | solution.py:258
  55.2 0.7 %copy.12 = bf16[8,128,128]{2,1,0:T(8,128)(2,1)} copy(bf16[8,128,128]{2,1,0:T(8,128)(2,1)S(1)} %get-tuple-element.4) | data formatting | bytes 524288
  55.9 0.7 %copy.13 = bf16[8,128,128]{2,1,0:T(8,128)(2,1)} copy(bf16[8,128,128]{2,1,0:T(8,128)(2,1)S(1)} %get-tuple-element.5) | data formatting | bytes 524288
Async XLA Ops:
  0.6 1.0 %copy-start = (bf16[8,128,128]{2,1,0:T(8,128)(2,1)S(1)}, bf16[8,128,128]{2,1,0:T(8,128)(2,1)}, u32[]{:S(2)}) copy-start(bf16[8,128,128]{2,1,0:T(8,128)(2,1)} %pair_ref.1) | copy-start | bytes 786436
  1.6 0.9 %copy-start.1 = (bf16[2,128,512]{2,1,0:T(8,128)(2,1)S(1)}, bf16[2,128,512]{2,1,0:T(8,128)(2,1)}, u32[]{:S(2)}) copy-start(bf16[2,128,512]{2,1,0:T(8,128)(2,1)} %w_in_ref.1) | copy-start | bytes 786436
  2.5 0.8 %copy-start.2 = (bf16[2,128,128]{2,1,0:T(8,128)(2,1)S(1)}, bf16[2,128,128]{2,1,0:T(8,128)(2,1)}, u32[]{:S(2)}) copy-start(bf16[2,128,128]{2,1,0:T(8,128)(2,1)} %w_gate_ref.1) | copy-start | bytes 196612
  3.4 0.8 %copy-start.3 = (bf16[2,128,128]{2,1,0:T(8,128)(2,1)S(1)}, bf16[2,128,128]{2,1,0:T(8,128)(2,1)}, u32[]{:S(2)}) copy-start(bf16[2,128,128]{2,1,0:T(8,128)(2,1)} %w_out_ref.1) | copy-start | bytes 196612
  4.2 0.7 %copy-start.4 = (f32[2,128]{1,0:T(2,128)S(1)}, f32[2,128]{1,0:T(2,128)}, u32[]{:S(2)}) copy-start(f32[2,128]{1,0:T(2,128)} %gain_in_ref.1) | copy-start | bytes 3076
  4.9 0.7 %copy-start.5 = (f32[2,128]{1,0:T(2,128)S(1)}, f32[2,128]{1,0:T(2,128)}, u32[]{:S(2)}) copy-start(f32[2,128]{1,0:T(2,128)} %bias_in_ref.1) | copy-start | bytes 3076
  5.6 0.7 %copy-start.6 = (f32[2,128]{1,0:T(2,128)S(1)}, f32[2,128]{1,0:T(2,128)}, u32[]{:S(2)}) copy-start(f32[2,128]{1,0:T(2,128)} %gain_mid_ref.1) | copy-start | bytes 3076
  6.3 0.7 %copy-start.7 = (f32[2,128]{1,0:T(2,128)S(1)}, f32[2,128]{1,0:T(2,128)}, u32[]{:S(2)}) copy-start(f32[2,128]{1,0:T(2,128)} %bias_mid_ref.1) | copy-start | bytes 3076

commit v2 on v0

--- a/solution.py
+++ b/solution.py
@@ -1,6 +1,10 @@
+import functools
+
 import jax
 import jax.numpy as jnp
 from jax import lax
+from jax.experimental import pallas as pl
+from jax.experimental.pallas import tpu as pltpu
 from jax.sharding import PartitionSpec as P
 
 
@@ -80,8 +84,246 @@
     final_state, middle = finish(pair_float, gate_values, returned, 1, w_out, gain_mid, bias_mid)
     return (final_state, middle.transpose(2, 0, 1))
 
+MESH = pl.DeviceIdType.MESH
+F32 = jnp.float32
+BF16 = jnp.bfloat16
+CHUNKS = 1
+VMEM_BYTES = 64 * 2**20 - 2**16
+
+
+def sigmoid(x):
+    return 0.5 * jnp.tanh(0.5 * x) + 0.5
+
+
+def norm_lanes(x, gain, bias):
+    center = jnp.mean(x, axis=-1, keepdims=True)
+    moved = x - center
+    spread = jnp.mean(moved * moved, axis=-1, keepdims=True)
+    return moved * lax.rsqrt(spread + 1e-05) * gain + bias
+
+
+def fused_kernel(
+    n,
+    chunks,
+    *refs,
+):
+    operands, refs = refs[:8], refs[8:]
+    out_ref, mid_ref = refs[:2]
+    loaded, refs = refs[2:10], refs[10:]
+    (
+        load_sem,
+        w_t,
+        state,
+        normed,
+        gate,
+        lanes_l,
+        lanes_r,
+        send_a,
+        recv_a,
+        send_b,
+        recv_b,
+        sa_sem,
+        ra_sem,
+        sb_sem,
+        rb_sem,
+    ) = refs
+    loads = [
+        pltpu.make_async_copy(src, dst, load_sem.at[k])
+        for k, (src, dst) in enumerate(zip(operands, loaded))
+    ]
+    for load in loads:
+        load.start()
+    (
+        pair_ref,
+        w_in_ref,
+        w_gate_ref,
+        w_out_ref,
+        gain_in_ref,
+        bias_in_ref,
+        gain_mid_ref,
+        bias_mid_ref,
+    ) = loaded
+    rows, tokens, channels = pair_ref.shape
+    hidden = w_out_ref.shape[1]
+    hb = hidden // n
+    part = hb * rows
+    per = hb // chunks
+    piece = per * rows
+    me = lax.axis_index("row")
+
+    barrier = pltpu.get_barrier_semaphore()
+
+    def greet(o, c):
+        pl.semaphore_signal(
+            barrier, inc=1, device_id={"row": lax.rem(me + o, n)}, device_id_type=MESH
+        )
+        return c
+
+    lax.fori_loop(1, n, greet, 0)
+
+    def start_all(bufs, k):
+        send, recv, ssem, rsem = bufs
+
+        def body(o, c):
+            other = lax.rem(me + o, n)
+            pltpu.make_async_remote_copy(
+                src_ref=send.at[k, other],
+                dst_ref=recv.at[k, me],
+                send_sem=ssem.at[k],
+                recv_sem=rsem.at[k],
+                device_id={"row": other},
+                device_id_type=MESH,
+            ).start()
+            return c
+
+        lax.fori_loop(1, n, body, 0)
+
+    def wait_all(bufs, k):
+        send, recv, ssem, rsem = bufs
+        blocks = recv.at[k, pl.ds(0, n - 1)]
+        pltpu.make_async_copy(blocks, blocks, rsem.at[k]).wait()
+
+    def drain(bufs, k):
+        send, recv, ssem, rsem = bufs
+        blocks = send.at[k, pl.ds(0, n - 1)]
+        pltpu.make_async_copy(blocks, blocks, ssem.at[k]).wait()
+
+    bufs_a = (send_a, recv_a, sa_sem, ra_sem)
+    bufs_b = (send_b, recv_b, sb_sem, rb_sem)
+
+    for k in (1, 4, 5, 0):
+        loads[k].wait()
+    w_t[0] = w_in_ref[0].T
+
+    for u in range(2):
+        source = pair_ref if u == 0 else state
+        for i in range(rows):
+            x = source[i].astype(F32)
+            nrm = norm_lanes(x, gain_in_ref[u : u + 1, :], bias_in_ref[u : u + 1, :]).astype(BF16)
+            normed[i] = nrm
+            proj = lax.dot_general(
+                w_t[u], nrm, (((1,), (1,)), ((), ())), preferred_element_type=F32
+            )
+            lanes_l[pl.ds(i, hidden, stride=rows), :] = (
+                sigmoid(proj[:hidden]) * proj[hidden : 2 * hidden]
+            )
+            lanes_r[pl.ds(i, hidden, stride=rows), :] = (
+                sigmoid(proj[2 * hidden : 3 * hidden]) * proj[3 * hidden :]
+            )
+        if u == 0:
+            pl.semaphore_wait(barrier, n - 1)
+        left = lanes_l[...].reshape(n, part, tokens)
+        right = lanes_r[...].reshape(n, part, tokens)
+        for c in range(chunks):
+            own = slice(c * piece, (c + 1) * piece)
+            send_a[u * chunks + c, :, :piece, :] = left[:, own].astype(BF16)
+            send_a[u * chunks + c, :, piece:, :] = right[:, own].astype(BF16)
+            start_all(bufs_a, u * chunks + c)
+        for c in range(chunks):
+            k = u * chunks + c
+            recv_a[k, pl.ds(me, 1)] = send_a[k, pl.ds(me, 1)]
+        if u == 0:
+            w_t[1] = w_in_ref[1].T
+            for k in (2, 3, 6, 7):
+                loads[k].wait()
+        for i in range(rows):
+            gate[i] = sigmoid(jnp.dot(normed[i], w_gate_ref[u], preferred_element_type=F32))
+        dims = (((1,), (1,)), ((), ())) if u == 0 else (((0,), (0,)), ((), ()))
+        for c in range(chunks):
+            k = u * chunks + c
+            wait_all(bufs_a, k)
+            for p in range(per // 2):
+                pair_of = slice(2 * p * rows, 2 * (p + 1) * rows)
+                lblk = recv_a[k, :, pair_of, :].astype(F32)
+                rblk = recv_a[k, :, piece + 2 * p * rows : piece + 2 * (p + 1) * rows, :].astype(F32)
+                tri = []
+                for q in range(2):
+                    cut = slice(q * rows, (q + 1) * rows)
+                    lh = lblk[:, cut, :].reshape(n * rows, tokens).astype(BF16)
+                    rh = rblk[:, cut, :].reshape(n * rows, tokens).astype(BF16)
+                    one = lax.dot_general(lh, rh, dims, preferred_element_type=F32)
+                    tri.append(one.reshape(n, rows, tokens))
+                send_b[k, :, pair_of, :] = jnp.concatenate(tri, axis=1).astype(BF16)
+            start_all(bufs_b, k)
+            recv_b[k, pl.ds(me, 1)] = send_b[k, pl.ds(me, 1)]
+        for c in range(chunks):
+            k = u * chunks + c
+            drain(bufs_a, k)
+            wait_all(bufs_b, k)
+            for d in range(n):
+                at = d * part + c * piece
+                lanes_l[at : at + piece, :] = recv_b[k, d].astype(F32)
+        for i in range(rows):
+            tri = lanes_l[pl.ds(i, hidden, stride=rows), :].T
+            mid = norm_lanes(
+                tri, gain_mid_ref[u : u + 1, :], bias_mid_ref[u : u + 1, :]
+            ).astype(BF16)
+            branch = jnp.dot(mid, w_out_ref[u], preferred_element_type=F32)
+            new = (source[i].astype(F32) + gate[i] * branch).astype(BF16)
+            if u == 0:
+                state[i] = new
+            else:
+                out_ref[i] = new
+                mid_ref[i] = mid
+    for k in range(2 * chunks):
+        drain(bufs_b, k)
+
+
+def fused(n, *operands):
+    pair, hidden = operands[0], operands[3].shape[1]
+    rows, tokens, channels = pair.shape
+    chunks = CHUNKS if hidden // n % (2 * CHUNKS) == 0 else 1
+    piece = hidden // n * rows // chunks
+    vmem = pl.BlockSpec(memory_space=pltpu.VMEM)
+    return pl.pallas_call(
+        functools.partial(fused_kernel, n, chunks),
+        out_shape=(
+            jax.ShapeDtypeStruct(pair.shape, BF16),
+            jax.ShapeDtypeStruct((rows, tokens, hidden), BF16),
+        ),
+        in_specs=[pl.BlockSpec(memory_space=pltpu.HBM)] * len(operands),
+        out_specs=(vmem, vmem),
+        scratch_shapes=[pltpu.VMEM(operand.shape, operand.dtype) for operand in operands]
+        + [
+            pltpu.SemaphoreType.DMA((len(operands),)),
+            pltpu.VMEM((2, 4 * hidden, channels), BF16),
+            pltpu.VMEM(pair.shape, BF16),
+            pltpu.VMEM(pair.shape, BF16),
+            pltpu.VMEM(pair.shape, F32),
+            pltpu.VMEM((hidden * rows, tokens), F32),
+            pltpu.VMEM((hidden * rows, tokens), F32),
+            pltpu.VMEM((2 * chunks, n, 2 * piece, tokens), BF16),
+            pltpu.VMEM((2 * chunks, n, 2 * piece, tokens), BF16),
+            pltpu.VMEM((2 * chunks, n, piece, tokens), BF16),
+            pltpu.VMEM((2 * chunks, n, piece, tokens), BF16),
+        ]
+        + [pltpu.SemaphoreType.DMA((2 * chunks,))] * 4,
+        compiler_params=pltpu.CompilerParams(
+            collective_id=0, has_side_effects=True, vmem_limit_bytes=VMEM_BYTES
+        ),
+    )(*operands)
+
+
+def fits(mesh, pair_shape, hidden):
+    n = mesh.shape["row"]
+    rows = pair_shape[0] // (n * mesh.shape["grp"])
+    tokens = pair_shape[1]
+    aligned = rows % 8 == 0 and hidden % (8 * n) == 0 and tokens % 128 == 0
+    small = hidden * rows * tokens * 40 <= 40 * 2**20
+    return mesh.shape["kc"] == 1 and n > 1 and n * rows == tokens and aligned and small
+
 
 def solution(mesh):
     in_specs = (P(("grp", "row"), "kc", None), P(), P(), P(), P(), P(), P(), P())
     out_specs = (P(("grp", "row"), "kc", None), P(("grp", "row"), "kc", None))
-    return jax.shard_map(shards, mesh=mesh, in_specs=in_specs, out_specs=out_specs, check_vma=False)
+
+    def run(*operands):
+        if fits(mesh, operands[0].shape, operands[3].shape[1]):
+            body = functools.partial(fused, mesh.shape["row"])
+        else:
+            body = shards
+        return jax.shard_map(
+            body, mesh=mesh, in_specs=in_specs, out_specs=out_specs, check_vma=False
+        )(*operands)
+
+    return run

time: 98.1 us -> 51.1 us (0.52)
  Pallas kernels: 0 us -> 47.8 us
  waiting for transfers between devices: 38.2 us -> 0 us
  blocking collectives: 25.6 us -> 0 us
  starting transfers between devices: 18 us -> 0 us
  local copies, waits for them, and re-layouts: 8.37 us -> 2.42 us
  matrix products: 3.9 us -> 0 us
  other arithmetic: 2.41 us -> 0 us
    pallas_call x0 -> x1, Pallas kernels: none -> 47.8 us  [fused(): pl.pallas_call(functools.partial(fused_kernel, n, chunks), out_shape=(jax...]
    all_to_all x4 -> x0, waiting for transfers between devices: 38.2 us -> none  [the longest x2 18.5 us: shards(): lax.all_to_all(summed.astype(jnp.bfloat16), 'row', split_axis=2, concat_a...]
    all_to_all x2 -> x0, blocking collectives: 25.6 us -> none  [the longest x1 12.8 us: shards(): lax.all_to_all(right, 'row', split_axis=0, concat_axis=1, tiled=True)]
    all_to_all x4 -> x0, starting transfers between devices: 18 us -> none  [the longest x1 7.36 us: shards(): lax.all_to_all(right, 'row', split_axis=0, concat_axis=1, tiled=True)]
    convert_element_type x9 -> x0, local copies, waits for them, and re-layouts: 4.06 us -> none  [the longest x2 1.07 us: prepare(): (jax.nn.sigmoid(projected[:hidden]) * projected[hidden:2 * hidden]).astyp...]
    dot_general x8 -> x0, matrix products: 3.9 us -> none  [the longest x2 1.98 us: prepare(): jnp.einsum('ijc,ch->hij', normed, w_in[layer_index], preferred_element_ty...]
    convert_element_type x6 -> x0, other arithmetic: 1.62 us -> none  [the longest x3 1.01 us: finish(): middle = layer_norm(returned.astype(jnp.float32), gain_mid[layer_index][:...]
    add x5 -> x0, local copies, waits for them, and re-layouts: 1.08 us -> none  [layer_norm(): return (values - center) * lax.rsqrt(spread + 1e-05) * gain + bias]
  transfers between devices with their start and end apart: 4 -> 0, of which waited for: 4 -> 0; matrix products, arithmetic and copies ran while one was open for 2% -> 0% of each run, Pallas kernels for 0% -> 0%
where the time goes in v2:
time: 51.1 us; the launch traced here: 50.9 us
  Pallas kernels  47.8 us (94%)
  local copies, waits for them, and re-layouts  2.42 us (5%)
  between operations  0.65 us (1%)
    pallas_call x1, Pallas kernels, fused(): pl.pallas_call(functools.partial(fused_kernel, n, chunks), out_shape=(jax...  47.8 us
    unnamed x4, local copies, waits for them, and re-layouts  2.42 us

profile of v2, /device:TPU:0, one launch (start us, length us, event | category | flops | bytes accessed | tf_op | source)
XLA Modules:
  0.0 50.9 jit_solution(14816742380786685700)
XLA Ops:
  0.6 47.8 %shard_map.95 = (bf16[8,128,128]{2,1,0:T(8,128)(2,1)}, bf16[8,128,128]{2,1,0:T(8,128)(2,1)}) custom-call(bf16[8,128,128]{2,1,0:T(8,128)(2,1)} %refs_0_.1, bf16[2,128,512]{2,1,0:T(8,128)(2,1)} %refs_1_.1, bf16[2,128,128]{2,1,0:T(8,128)(2,1)} %refs_2_.1, bf16[2,128,128]{2,1,0:T(8,128)(2,1)} %refs_3_.1, f32[2,128]{1,0:T(2,128)} %refs_4_.1, f32[2,128]{1,0:T(2,128)} %refs_5_.1, ...), custom_call_target="tpu_custom_call" | custom-call | tf_op jit(solution)/shard_map/pallas_call | solution.py:278
  48.5 0.0 copy-start
  48.5 1.7 %copy.12 = bf16[8,128,128]{2,1,0:T(8,128)(2,1)} copy(bf16[8,128,128]{2,1,0:T(8,128)(2,1)} %get-tuple-element.4) | data formatting | bytes 524288
  50.2 0.0 copy-done
  50.2 0.7 %copy.13 = bf16[8,128,128]{2,1,0:T(8,128)(2,1)} copy(bf16[8,128,128]{2,1,0:T(8,128)(2,1)S(1)} %copy-done) | data formatting | bytes 524288
Async XLA Ops:
  48.5 1.7 %copy-start = (bf16[8,128,128]{2,1,0:T(8,128)(2,1)S(1)}, bf16[8,128,128]{2,1,0:T(8,128)(2,1)}, u32[]{:S(2)}) copy-start(bf16[8,128,128]{2,1,0:T(8,128)(2,1)} %get-tuple-element.5) | copy-start | bytes 786436

commit v3 on v2

--- a/solution.py
+++ b/solution.py
@@ -161,11 +161,18 @@
 
     lax.fori_loop(1, n, greet, 0)
 
-    def start_all(bufs, k):
+    flips = []
+    for bit in range(n.bit_length() - 1):
+        size = 2**bit
+        flips.append(size - 2 * size * lax.rem(lax.div(me, size), 2))
+
+    def start_all(bufs, k, offsets):
         send, recv, ssem, rsem = bufs
-
-        def body(o, c):
-            other = lax.rem(me + o, n)
+        for o in offsets:
+            other = me
+            for bit, flip in enumerate(flips):
+                if o // 2**bit % 2 == 1:
+                    other = other + flip
             pltpu.make_async_remote_copy(
                 src_ref=send.at[k, other],
                 dst_ref=recv.at[k, me],
@@ -174,9 +181,6 @@
                 device_id={"row": other},
                 device_id_type=MESH,
             ).start()
-            return c
-
-        lax.fori_loop(1, n, body, 0)
 
     def wait_all(bufs, k):
         send, recv, ssem, rsem = bufs
@@ -199,26 +203,33 @@
         source = pair_ref if u == 0 else state
         for i in range(rows):
             x = source[i].astype(F32)
-            nrm = norm_lanes(x, gain_in_ref[u : u + 1, :], bias_in_ref[u : u + 1, :]).astype(BF16)
-            normed[i] = nrm
-            proj = lax.dot_general(
-                w_t[u], nrm, (((1,), (1,)), ((), ())), preferred_element_type=F32
+            normed[i] = norm_lanes(
+                x, gain_in_ref[u : u + 1, :], bias_in_ref[u : u + 1, :]
+            ).astype(BF16)
+        half, wide = n // 2, hidden // 2
+        own_half = lax.div(me, half)
+        for stage, side in enumerate((1 - own_half, own_half)):
+            first = pl.multiple_of(side * wide, wide)
+            weights = jnp.concatenate(
+                [w_t[u, pl.ds(g * hidden + first, wide), :] for g in range(4)], axis=0
             )
-            lanes_l[pl.ds(i, hidden, stride=rows), :] = (
-                sigmoid(proj[:hidden]) * proj[hidden : 2 * hidden]
-            )
-            lanes_r[pl.ds(i, hidden, stride=rows), :] = (
-                sigmoid(proj[2 * hidden : 3 * hidden]) * proj[3 * hidden :]
-            )
-        if u == 0:
-            pl.semaphore_wait(barrier, n - 1)
-        left = lanes_l[...].reshape(n, part, tokens)
-        right = lanes_r[...].reshape(n, part, tokens)
-        for c in range(chunks):
-            own = slice(c * piece, (c + 1) * piece)
-            send_a[u * chunks + c, :, :piece, :] = left[:, own].astype(BF16)
-            send_a[u * chunks + c, :, piece:, :] = right[:, own].astype(BF16)
-            start_all(bufs_a, u * chunks + c)
+            base = stage * wide * rows
+            for i in range(rows):
+                proj = lax.dot_general(
+                    weights, normed[i], (((1,), (1,)), ((), ())), preferred_element_type=F32
+                )
+                at = pl.ds(base + i, wide, stride=rows)
+                lanes_l[at, :] = sigmoid(proj[:wide]) * proj[wide : 2 * wide]
+                lanes_r[at, :] = sigmoid(proj[2 * wide : 3 * wide]) * proj[3 * wide :]
+            owners = pl.ds(side * half, half)
+            part_of = slice(base, base + wide * rows)
+            left = lanes_l[part_of, :].reshape(half, part, tokens)
+            right = lanes_r[part_of, :].reshape(half, part, tokens)
+            send_a[u, owners, :part, :] = left.astype(BF16)
+            send_a[u, owners, part:, :] = right.astype(BF16)
+            if u == 0 and stage == 0:
+                pl.semaphore_wait(barrier, n - 1)
+            start_all(bufs_a, u, range(n - 1, half - 1, -1) if stage == 0 else range(half - 1, 0, -1))
         for c in range(chunks):
             k = u * chunks + c
             recv_a[k, pl.ds(me, 1)] = send_a[k, pl.ds(me, 1)]
@@ -244,7 +255,7 @@
                     one = lax.dot_general(lh, rh, dims, preferred_element_type=F32)
                     tri.append(one.reshape(n, rows, tokens))
                 send_b[k, :, pair_of, :] = jnp.concatenate(tri, axis=1).astype(BF16)
-            start_all(bufs_b, k)
+            start_all(bufs_b, k, range(n - 1, 0, -1))
             recv_b[k, pl.ds(me, 1)] = send_b[k, pl.ds(me, 1)]
         for c in range(chunks):
             k = u * chunks + c
@@ -310,7 +321,7 @@
     tokens = pair_shape[1]
     aligned = rows % 8 == 0 and hidden % (8 * n) == 0 and tokens % 128 == 0
     small = hidden * rows * tokens * 40 <= 40 * 2**20
-    return mesh.shape["kc"] == 1 and n > 1 and n * rows == tokens and aligned and small
+    return mesh.shape["kc"] == 1 and n > 1 and n & (n - 1) == 0 and n * rows == tokens and aligned and small
 
 
 def solution(mesh):

time: 51.1 us -> 50 us (0.978)
  Pallas kernels: 47.8 us -> 46.8 us
    pallas_call x1, Pallas kernels: 47.8 us -> 46.8 us  [fused(): pl.pallas_call(functools.partial(fused_kernel, n, chunks), out_shape=(jax...]
where the time goes in v3:
time: 50 us; the launch traced here: 49.8 us
  Pallas kernels  46.8 us (94%)
  local copies, waits for them, and re-layouts  2.42 us (5%)
  between operations  0.65 us (1%)
    pallas_call x1, Pallas kernels, fused(): pl.pallas_call(functools.partial(fused_kernel, n, chunks), out_shape=(jax...  46.8 us
    unnamed x4, local copies, waits for them, and re-layouts  2.42 us

profile of v3, /device:TPU:0, one launch (start us, length us, event | category | flops | bytes accessed | tf_op | source)
XLA Modules:
  0.0 49.8 jit_solution(6304329364679838037)
XLA Ops:
  0.6 46.8 %shard_map.95 = (bf16[8,128,128]{2,1,0:T(8,128)(2,1)}, bf16[8,128,128]{2,1,0:T(8,128)(2,1)}) custom-call(bf16[8,128,128]{2,1,0:T(8,128)(2,1)} %refs_0_.1, bf16[2,128,512]{2,1,0:T(8,128)(2,1)} %refs_1_.1, bf16[2,128,128]{2,1,0:T(8,128)(2,1)} %refs_2_.1, bf16[2,128,128]{2,1,0:T(8,128)(2,1)} %refs_3_.1, f32[2,128]{1,0:T(2,128)} %refs_4_.1, f32[2,128]{1,0:T(2,128)} %refs_5_.1, ...), custom_call_target="tpu_custom_call" | custom-call | tf_op jit(solution)/shard_map/pallas_call | solution.py:289
  47.4 0.0 copy-start
  47.4 1.7 %copy.12 = bf16[8,128,128]{2,1,0:T(8,128)(2,1)} copy(bf16[8,128,128]{2,1,0:T(8,128)(2,1)} %get-tuple-element.4) | data formatting | bytes 524288
  49.1 0.0 copy-done
  49.1 0.7 %copy.13 = bf16[8,128,128]{2,1,0:T(8,128)(2,1)} copy(bf16[8,128,128]{2,1,0:T(8,128)(2,1)S(1)} %copy-done) | data formatting | bytes 524288
Async XLA Ops:
  47.4 1.7 %copy-start = (bf16[8,128,128]{2,1,0:T(8,128)(2,1)S(1)}, bf16[8,128,128]{2,1,0:T(8,128)(2,1)}, u32[]{:S(2)}) copy-start(bf16[8,128,128]{2,1,0:T(8,128)(2,1)} %get-tuple-element.5) | copy-start | bytes 786436

commit v4 on v3

--- a/solution.py
+++ b/solution.py
@@ -315,11 +315,54 @@
     )(*operands)
 
 
+def store_kernel(new_ref, mid_ref, out_ref, out_mid_ref, held, sem_in, sem_out):
+    pieces = held.shape[1]
+    moves = []
+    for which, (src, dst) in enumerate(((new_ref, out_ref), (mid_ref, out_mid_ref))):
+        size = src.shape[0] // pieces
+        for p in range(pieces):
+            at = pl.ds(p * size, size)
+            moves.append(
+                (
+                    pltpu.make_async_copy(src.at[at], held.at[which, p], sem_in.at[which, p]),
+                    pltpu.make_async_copy(held.at[which, p], dst.at[at], sem_out.at[which, p]),
+                )
+            )
+    for load, _ in moves:
+        load.start()
+    for load, save in moves:
+        load.wait()
+        save.start()
+    for _, save in moves:
+        save.wait()
+
+
+def store(new, mid):
+    hbm = pl.BlockSpec(memory_space=pltpu.HBM)
+    pieces = 2
+    return pl.pallas_call(
+        store_kernel,
+        out_shape=(
+            jax.ShapeDtypeStruct(new.shape, new.dtype),
+            jax.ShapeDtypeStruct(mid.shape, mid.dtype),
+        ),
+        in_specs=[hbm, hbm],
+        out_specs=(hbm, hbm),
+        scratch_shapes=[
+            pltpu.VMEM((2, pieces, new.shape[0] // pieces) + new.shape[1:], new.dtype),
+            pltpu.SemaphoreType.DMA((2, pieces)),
+            pltpu.SemaphoreType.DMA((2, pieces)),
+        ],
+        compiler_params=pltpu.CompilerParams(vmem_limit_bytes=VMEM_BYTES),
+    )(new, mid)
+
+
 def fits(mesh, pair_shape, hidden):
     n = mesh.shape["row"]
     rows = pair_shape[0] // (n * mesh.shape["grp"])
     tokens = pair_shape[1]
     aligned = rows % 8 == 0 and hidden % (8 * n) == 0 and tokens % 128 == 0
+    aligned = aligned and hidden == pair_shape[2]
     small = hidden * rows * tokens * 40 <= 40 * 2**20
     return mesh.shape["kc"] == 1 and n > 1 and n & (n - 1) == 0 and n * rows == tokens and aligned and small
 
@@ -330,7 +373,11 @@
 
     def run(*operands):
         if fits(mesh, operands[0].shape, operands[3].shape[1]):
-            body = functools.partial(fused, mesh.shape["row"])
+            n = mesh.shape["row"]
+
+            def body(*local):
+                return store(*fused(n, *local))
+
         else:
             body = shards
         return jax.shard_map(

time: 50 us -> 49.4 us (0.988)
  local copies, waits for them, and re-layouts: 2.42 us -> 0 us
  Pallas kernels: 46.8 us -> 48.6 us
    unnamed x4 -> x0, local copies, waits for them, and re-layouts: 2.42 us -> none
    pallas_call x0 -> x1, Pallas kernels: none -> 1.82 us  [store(): pl.pallas_call(store_kernel, out_shape=(jax.ShapeDtypeStruct(new.shape, n...]
where the time goes in v4:
time: 49.4 us; the launch traced here: 49.2 us
  Pallas kernels  48.6 us (98%)
  between operations  0.64 us (1%)
    pallas_call x1, Pallas kernels, fused(): pl.pallas_call(functools.partial(fused_kernel, n, chunks), out_shape=(jax...  46.8 us
    pallas_call x1, Pallas kernels, store(): pl.pallas_call(store_kernel, out_shape=(jax.ShapeDtypeStruct(new.shape, n...  1.82 us

profile of v4, /device:TPU:0, one launch (start us, length us, event | category | flops | bytes accessed | tf_op | source)
XLA Modules:
  0.0 49.2 jit_solution(3328251278067741287)
XLA Ops:
  0.6 46.8 %shard_map.95 = (bf16[8,128,128]{2,1,0:T(8,128)(2,1)}, bf16[8,128,128]{2,1,0:T(8,128)(2,1)}) custom-call(bf16[8,128,128]{2,1,0:T(8,128)(2,1)} %refs_0_.1, bf16[2,128,512]{2,1,0:T(8,128)(2,1)} %refs_1_.1, bf16[2,128,128]{2,1,0:T(8,128)(2,1)} %refs_2_.1, bf16[2,128,128]{2,1,0:T(8,128)(2,1)} %refs_3_.1, f32[2,128]{1,0:T(2,128)} %refs_4_.1, f32[2,128]{1,0:T(2,128)} %refs_5_.1, ...), custom_call_target="tpu_custom_call" | custom-call | tf_op jit(solution)/shard_map/pallas_call | solution.py:289
  47.4 1.8 %shard_map.96 = (bf16[8,128,128]{2,1,0:T(8,128)(2,1)}, bf16[8,128,128]{2,1,0:T(8,128)(2,1)}) custom-call(bf16[8,128,128]{2,1,0:T(8,128)(2,1)} %get-tuple-element.4.new_ref, bf16[8,128,128]{2,1,0:T(8,128)(2,1)} %get-tuple-element.5.mid_ref), custom_call_target="tpu_custom_call" | custom-call | tf_op jit(solution)/shard_map/pallas_call | solution.py:343

commit v5 on v4

--- a/solution.py
+++ b/solution.py
@@ -126,7 +126,11 @@
         ra_sem,
         sb_sem,
         rb_sem,
+        out_buf,
+        mid_buf,
+        save_sem,
     ) = refs
+    pending = []
     loads = [
         pltpu.make_async_copy(src, dst, load_sem.at[k])
         for k, (src, dst) in enumerate(zip(operands, loaded))
@@ -260,6 +264,8 @@
         for c in range(chunks):
             k = u * chunks + c
             drain(bufs_a, k)
+            if u == 1:
+                drain(bufs_b, c)
             wait_all(bufs_b, k)
             for d in range(n):
                 at = d * part + c * piece
@@ -274,9 +280,18 @@
             if u == 0:
                 state[i] = new
             else:
-                out_ref[i] = new
-                mid_ref[i] = mid
-    for k in range(2 * chunks):
+                out_buf[i] = new
+                mid_buf[i] = mid
+                saves = [
+                    pltpu.make_async_copy(out_buf.at[i], out_ref.at[i], save_sem.at[0, i]),
+                    pltpu.make_async_copy(mid_buf.at[i], mid_ref.at[i], save_sem.at[1, i]),
+                ]
+                for save in saves:
+                    save.start()
+                pending.extend(saves)
+    for save in pending:
+        save.wait()
+    for k in range(chunks, 2 * chunks):
         drain(bufs_b, k)
 
 
@@ -293,7 +308,7 @@
             jax.ShapeDtypeStruct((rows, tokens, hidden), BF16),
         ),
         in_specs=[pl.BlockSpec(memory_space=pltpu.HBM)] * len(operands),
-        out_specs=(vmem, vmem),
+        out_specs=(pl.BlockSpec(memory_space=pltpu.HBM),) * 2,
         scratch_shapes=[pltpu.VMEM(operand.shape, operand.dtype) for operand in operands]
         + [
             pltpu.SemaphoreType.DMA((len(operands),)),
@@ -308,7 +323,12 @@
             pltpu.VMEM((2 * chunks, n, piece, tokens), BF16),
             pltpu.VMEM((2 * chunks, n, piece, tokens), BF16),
         ]
-        + [pltpu.SemaphoreType.DMA((2 * chunks,))] * 4,
+        + [pltpu.SemaphoreType.DMA((2 * chunks,))] * 4
+        + [
+            pltpu.VMEM(pair.shape, BF16),
+            pltpu.VMEM((rows, tokens, hidden), BF16),
+            pltpu.SemaphoreType.DMA((2, rows)),
+        ],
         compiler_params=pltpu.CompilerParams(
             collective_id=0, has_side_effects=True, vmem_limit_bytes=VMEM_BYTES
         ),

time: 49.4 us -> 49.4 us (level)
  no operation moved by 1% of the time
where the time goes in v5:
time: 49.4 us; the launch traced here: 49.2 us
  Pallas kernels  48.6 us (98%)
  between operations  0.64 us (1%)
    pallas_call x1, Pallas kernels, fused(): pl.pallas_call(functools.partial(fused_kernel, n, chunks), out_shape=(jax...  46.8 us
    pallas_call x1, Pallas kernels, store(): pl.pallas_call(store_kernel, out_shape=(jax.ShapeDtypeStruct(new.shape, n...  1.82 us

profile of v5, /device:TPU:0, one launch (start us, length us, event | category | flops | bytes accessed | tf_op | source)
XLA Modules:
  0.0 49.2 jit_solution(3574404128822746765)
XLA Ops:
  0.6 46.8 %shard_map.95 = (bf16[8,128,128]{2,1,0:T(8,128)(2,1)}, bf16[8,128,128]{2,1,0:T(8,128)(2,1)}) custom-call(bf16[8,128,128]{2,1,0:T(8,128)(2,1)} %refs_0_.1, bf16[2,128,512]{2,1,0:T(8,128)(2,1)} %refs_1_.1, bf16[2,128,128]{2,1,0:T(8,128)(2,1)} %refs_2_.1, bf16[2,128,128]{2,1,0:T(8,128)(2,1)} %refs_3_.1, f32[2,128]{1,0:T(2,128)} %refs_4_.1, f32[2,128]{1,0:T(2,128)} %refs_5_.1, ...), custom_call_target="tpu_custom_call" | custom-call | tf_op jit(solution)/shard_map/pallas_call | solution.py:304
  47.4 1.8 %shard_map.96 = (bf16[8,128,128]{2,1,0:T(8,128)(2,1)}, bf16[8,128,128]{2,1,0:T(8,128)(2,1)}) custom-call(bf16[8,128,128]{2,1,0:T(8,128)(2,1)} %get-tuple-element.4.new_ref, bf16[8,128,128]{2,1,0:T(8,128)(2,1)} %get-tuple-element.5.mid_ref), custom_call_target="tpu_custom_call" | custom-call | tf_op jit(solution)/shard_map/pallas_call | solution.py:363
